TPU v7x, 256 devices: a whole 4x4x8 slice. The times are simulated.
256 devices in a mesh: seq: 64 (over z, y, core), chan: 4 (over x).
Axes of the slice: x: 4, y: 4, z: 8, core: 2. Of those that a mesh axis runs over, the one named last changes fastest.
Arguments:
- residual: bfloat16 [8192, 8192], P('seq', 'chan'), may hold values from -6 to 6
- hyena_q: bfloat16 [8192, 8192], P('seq', 'chan'), may hold values from -6 to 6
- hyena_k: bfloat16 [8192, 8192], P('seq', 'chan'), may hold values from -6 to 6
- hyena_v: bfloat16 [8192, 8192], P('seq', 'chan'), may hold values from -6 to 6
- modal_residue: float32 [8192, 16], P('chan'), may hold values from -0.06 to 0.06
- decay_rate: float32 [8192, 16], P('chan'), may hold values from 6.1035156e-05 to 0.05
- skip_gain: float32 [8192], P('chan'), may hold values from -1 to 1
- attn_q: bfloat16 [8192, 8192], P('seq', 'chan'), may hold values from -6 to 6
- attn_k: bfloat16 [8192, 8192], P('seq', 'chan'), may hold values from -6 to 6
- norm_gain: float32 [8192], P('chan'), may hold values from 0.5 to 1.5
- readers: int32 [64, 64], P('seq'), may hold values from -1 to 7, as said below
Outputs:
- block_out: bfloat16 [8192, 8192], P('seq', 'chan')
Inputs may be any that keep to these rules, and one draw needn't show every extreme that they name: readers[q, j] is -1 whenever j >= q; otherwise -1 or a tile index below 8.
All inputs are finite; a program needn't handle non-finite values.
Results may differ from a plain program's by a relative error of at most 0.0052.
Values may be sent and summed in bfloat16 or wider, within the bound.
A program may use at most 256 MiB of HBM per device.

v0:
```python
from functools import partial

import jax
import jax.numpy as jnp
from jax import lax
from jax.sharding import PartitionSpec as P

HEAD_DIM = 128
TILE = 16


def link_states(earlier, later):
    return (later[0] + later[1] * earlier[0], earlier[1] * later[1])


def modal_group(operands):
    signal, residue, rates = operands
    length, width = signal.shape
    count = length // 128
    offsets = jnp.arange(128, dtype=jnp.float32)
    kernel = jnp.einsum(
        "gm,gmd->gd",
        residue,
        jnp.exp(-rates[:, :, None] * offsets),
        precision=lax.Precision.HIGHEST,
    )
    spread = jnp.arange(128)[:, None] - jnp.arange(128)[None, :]
    toeplitz = jnp.where(spread[None] >= 0, kernel[:, jnp.clip(spread, 0)], 0.0)
    blocks = signal.reshape(count, 128, width)
    inner = jnp.einsum("gij,njg->nig", toeplitz, blocks, precision=lax.Precision.HIGHEST)
    tail = jnp.exp(-rates[:, :, None] * (127.0 - offsets))
    ends = jnp.einsum("gmj,njg->ngm", tail, blocks, precision=lax.Precision.HIGHEST)
    stepped = jnp.broadcast_to(jnp.exp(-rates * 128.0)[None], ends.shape)
    states, _ = lax.associative_scan(link_states, (ends, stepped), axis=0)
    before = jnp.concatenate([jnp.zeros_like(states[:1]), states[:-1]], axis=0)
    lead = residue[:, :, None] * jnp.exp(-rates[:, :, None] * (offsets + 1.0))
    outer = jnp.einsum("gmi,ngm->nig", lead, before, precision=lax.Precision.HIGHEST)
    return ((inner + outer).reshape(length, width), states[-1])


def modal_conv(signal, residue, rates):
    length, channels = signal.shape
    width = min(channels, 128)
    groups = channels // width
    stacked = signal.reshape(length, groups, width).transpose(1, 0, 2)
    outputs, finals = lax.map(
        modal_group, (stacked, residue.reshape(groups, width, -1), rates.reshape(groups, width, -1))
    )
    return (outputs.transpose(1, 0, 2).reshape(length, channels), finals.reshape(channels, -1))


def split_heads(array):
    rows, features = array.shape
    return array.reshape(rows, features // HEAD_DIM, HEAD_DIM).transpose(1, 0, 2)


def head_partial(allowed, operands):
    queries, keys, values = operands
    scores = jnp.einsum("qd,kd->qk", queries, keys, preferred_element_type=jnp.float32) / jnp.sqrt(
        jnp.float32(HEAD_DIM)
    )
    scores = jnp.where(allowed, scores, -1e30)
    peak = jnp.max(scores, axis=1)
    weights = jnp.where(allowed, jnp.exp(scores - peak[:, None]), 0.0)
    total = jnp.sum(weights, axis=1)
    summed = jnp.dot(weights.astype(jnp.bfloat16), values, preferred_element_type=jnp.float32)
    return (peak, total, summed)


def local(
    residual,
    hyena_q,
    hyena_k,
    hyena_v,
    modal_residue,
    decay_rate,
    skip_gain,
    attn_q,
    attn_k,
    norm_gain,
    readers,
):
    product = (hyena_k.astype(jnp.float32) * hyena_v.astype(jnp.float32)).astype(jnp.bfloat16)
    shards = lax.axis_size("seq")
    my_index = lax.axis_index("seq")
    columns = product.shape[1] // shards
    gathered = lax.all_to_all(product, "seq", split_axis=1, concat_axis=0, tiled=True)
    first_col = my_index * columns
    residue_part = lax.dynamic_slice_in_dim(modal_residue, first_col, columns, 0)
    rate_part = lax.dynamic_slice_in_dim(decay_rate, first_col, columns, 0)
    skip_part = lax.dynamic_slice_in_dim(skip_gain, first_col, columns, 0)
    whole_signal = gathered.astype(jnp.float32)
    filtered, _ = modal_conv(whole_signal, residue_part, rate_part)
    mixed = (filtered + skip_part[None, :] * whole_signal).astype(jnp.bfloat16)
    convolved = lax.all_to_all(mixed, "seq", split_axis=0, concat_axis=1, tiled=True)
    stream = residual.astype(jnp.float32) + hyena_q.astype(jnp.float32) * convolved.astype(
        jnp.float32
    )
    squares = jnp.sum(stream * stream, axis=1)
    total_sq = lax.psum(squares, "chan")
    width_all = stream.shape[1] * lax.axis_size("chan")
    values = (
        stream * lax.rsqrt(total_sq / width_all + 1e-06)[:, None] * norm_gain[None, :]
    ).astype(jnp.bfloat16)
    tok_rows, features = attn_q.shape
    my_reads = readers[0]
    shard_count = my_reads.shape[0]
    query_heads = split_heads(attn_q)
    causal = jnp.tril(jnp.ones((tok_rows, tok_rows), bool))
    asked = lax.all_to_all(readers, "seq", split_axis=1, concat_axis=0, tiled=True)[:, 0]
    chosen = jnp.clip(asked, 0)
    send_keys = jnp.take(attn_k.reshape(-1, TILE, features), chosen, axis=0)
    send_values = jnp.take(values.reshape(-1, TILE, features), chosen, axis=0)
    got_keys, got_values = (
        lax.all_to_all(send_keys, "seq", split_axis=0, concat_axis=0, tiled=True),
        lax.all_to_all(send_values, "seq", split_axis=0, concat_axis=0, tiled=True),
    )
    all_keys = jnp.concatenate([attn_k, got_keys.reshape(-1, features)], axis=0)
    all_values = jnp.concatenate([values, got_values.reshape(-1, features)], axis=0)
    remote_ok = jnp.broadcast_to(
        jnp.repeat(my_reads >= 0, TILE)[None, :], (tok_rows, shard_count * TILE)
    )
    allowed = jnp.concatenate([causal, remote_ok], axis=1)
    peak, total, summed = lax.map(
        partial(head_partial, allowed),
        (query_heads, split_heads(all_keys), split_heads(all_values)),
    )
    attended = (summed / total[..., None]).transpose(1, 0, 2).reshape(tok_rows, features)
    return (stream + attended).astype(jnp.bfloat16)


def solution(mesh):
    placed = (
        P("seq", "chan"),
        P("seq", "chan"),
        P("seq", "chan"),
        P("seq", "chan"),
        P("chan", None),
        P("chan", None),
        P("chan"),
        P("seq", "chan"),
        P("seq", "chan"),
        P("chan"),
        P("seq", None),
    )
    return jax.shard_map(
        local, mesh=mesh, in_specs=placed, out_specs=P("seq", "chan"), check_vma=False
    )
```

profile of v0, /device:TPU:1, one launch (start us, length us, event | category | flops | bytes accessed | tf_op | source)
XLA Modules:
  0.0 579.8 jit_solution(15403880521795649169)
XLA Ops:
  3.6 13.2 %all-to-all-start = ((bf16[128,64,32]{0,2,1:T(8,128)(2,1)}), bf16[128,64,32]{0,2,1:T(8,128)(2,1)S(1)}, u32[]{:S(2)}, u32[]{:S(2)}) async-start(bf16[128,64,32]{0,2,1:T(8,128)(2,1)} %bitcast.5), calls=%async_computation | async-start | bytes 1048576 | tf_op jit(solution)/shard_map/all_to_all | solution.py:87
  20.8 54.4 %gather_fusion = f32[16384,32]{1,0:T(8,128)} fusion(f32[32,128]{0,1:T(8,128)S(1)} %copy.190, s32[16384]{0:T(1024)S(1)} %bitcast_clamp_fusion), kind=kCustom, calls=%fused_computation.2 | custom fusion | bytes 4259840 | tf_op jit(solution)/shard_map/while/body/eval_jaxpr/gather | solution.py:28
  75.3 5.5 copy.159
  83.4 10.3 %all-to-all-start.2 = ((s32[1,64,1]{2,0,1:T(1,128)}), s32[1,64,1]{2,0,1:T(1,128)S(1)}, u32[]{:S(2)}, u32[]{:S(2)}) async-start(s32[1,64,1]{2,0,1:T(1,128)} %copy.178), calls=%async_computation.2 | async-start | bytes 65536 | tf_op jit(solution)/shard_map/all_to_all | solution.py:110
  94.7 3.3 slice.174
  98.0 3.7 slice.176
  102.8 1.9 slice.180
  104.7 2.4 slice.182
  109.3 1.9 slice.188
  112.3 1.7 slice.192
  114.0 1.6 slice.194
  119.9 1.6 slice.190
  121.5 1.9 slice.184
  123.4 2.3 slice.178
  125.7 3.7 slice.172
  132.5 1.9 fusion.60
  134.4 12.4 %pad.53 = f32[4,32,16]{0,2,1:T(8,128)S(1)} pad(f32[2,32,16]{0,2,1:T(8,128)} %pad_add_fusion.1, f32[]{:T(128)} %constant.59.clone.1), padding=1_0_1x0_0_0x0_0_0 | pad | bytes 12292 | tf_op jit(solution)/shard_map/while/body/eval_jaxpr/pad | solution.py:34
  146.8 1.9 pad_maximum_fusion
  148.6 15.9 %pad.52 = f32[4,32,16]{0,2,1:T(8,128)} pad(f32[2,32,16]{0,2,1:T(8,128)} %pad_maximum_fusion, f32[]{:T(128)} %constant.59.clone.1), padding=0_1_1x0_0_0x0_0_0 | pad | bytes 12292 | tf_op jit(solution)/shard_map/while/body/eval_jaxpr/pad | solution.py:34
  164.5 1.7 add.154
  167.5 2.4 pad.54
  169.8 12.4 %pad.55 = f32[8,32,16]{0,2,1:T(8,128)S(1)} pad(f32[4,32,16]{0,2,1:T(8,128)} %add.154, f32[]{:T(128)} %constant.59.clone.1), padding=1_0_1x0_0_0x0_0_0 | pad | bytes 24580 | tf_op jit(solution)/shard_map/while/body/eval_jaxpr/pad | solution.py:34
  183.7 12.6 %pad.57 = f32[16,32,16]{0,2,1:T(8,128)S(1)} pad(f32[8,32,16]{0,2,1:T(8,128)} %add.156, f32[]{:T(128)} %constant.59.clone.1), padding=1_0_1x0_0_0x0_0_0 | pad | bytes 49156 | tf_op jit(solution)/shard_map/while/body/eval_jaxpr/pad | solution.py:34
  197.6 2.7 pad.56
  203.0 12.8 %pad.58 = f32[32,32,16]{0,2,1:T(8,128)S(1)} pad(f32[16,32,16]{0,2,1:T(8,128)} %pad_maximum_fusion.3, f32[]{:T(128)} %constant.59.clone.1), padding=0_1_1x0_0_0x0_0_0 | pad | bytes 98308 | tf_op jit(solution)/shard_map/while/body/eval_jaxpr/pad | solution.py:34
  215.8 12.8 %pad.59 = f32[32,32,16]{0,2,1:T(8,128)S(1)} pad(f32[16,32,16]{0,2,1:T(8,128)} %add.158, f32[]{:T(128)} %constant.59.clone.1), padding=1_0_1x0_0_0x0_0_0 | pad | bytes 98308 | tf_op jit(solution)/shard_map/while/body/eval_jaxpr/pad | solution.py:34
  229.4 16.6 %pad.104 = f32[64,32,16]{0,2,1:T(8,128)} pad(f32[32,32,16]{0,2,1:T(8,128)} %add.160, f32[]{:T(128)} %constant.59.clone.1), padding=1_0_1x0_0_0x0_0_0 | pad | bytes 196612
  247.2 4.5 pad.82
  252.7 2.1 fusion.42
  254.8 2.1 fusion.28
  258.0 10.3 %all-to-all-start.1 = ((bf16[64,128,32]{1,2,0:T(8,128)(2,1)}), bf16[64,128,32]{1,2,0:T(8,128)(2,1)S(1)}, u32[]{:S(2)}, u32[]{:S(2)}) async-start(bf16[64,128,32]{1,2,0:T(8,128)(2,1)} %copy.175), calls=%async_computation.1 | async-start | bytes 1048576 | tf_op jit(solution)/shard_map/all_to_all | solution.py:95
  272.2 2.8 gather_fusion.1
  275.0 11.0 %all-to-all-done.1 = bf16[64,128,32]{1,2,0:T(8,128)(2,1)S(1)} async-done(((bf16[64,128,32]{1,2,0:T(8,128)(2,1)}), bf16[64,128,32]{1,2,0:T(8,128)(2,1)S(1)}, u32[]{:S(2)}, u32[]{:S(2)}) %all-to-all-start.1) | async-done | bytes 524320 | tf_op jit(solution)/shard_map/all_to_all | solution.py:95
  286.3 8.5 %psum.7 = f32[128]{0:T(128)S(1)} all-reduce(f32[128]{0:T(128)S(1)} %multiply_reduce_fusion), channel_id=1, replica_groups=mesh['seq'=64,'chan'=4] {'chan'}, use_global_device_ids=true, to_apply=%region_1.3 | all-reduce | flops 128 | bytes 1024 | tf_op jit(solution)/shard_map/psum | solution.py:100
  295.4 2.8 gather_fusion.2
  298.2 5.3 broadcast_select_fusion
  303.5 102.2 %all_to_all.46 = bf16[64,16,2048]{2,1,0:T(8,128)(2,1)} all-to-all(bf16[64,16,2048]{2,1,0:T(8,128)(2,1)S(1)} %get-tuple-element.124), channel_id=1, replica_groups=mesh['seq'=64,'chan'=4] {'seq'}, dimensions={0} | all-to-all | bytes 8388608 | tf_op jit(solution)/shard_map/all_to_all | solution.py:116
  405.7 7.4 %all-to-all-start.3 = ((bf16[64,16,2048]{2,1,0:T(8,128)(2,1)}), bf16[64,16,2048]{2,1,0:T(8,128)(2,1)}, u32[]{:S(2)}, u32[]{:S(2)}) async-start(bf16[64,16,2048]{2,1,0:T(8,128)(2,1)} %get-tuple-element.125), calls=%async_computation.3 | async-start | bytes 8388608 | tf_op jit(solution)/shard_map/all_to_all | solution.py:115
  415.6 2.0 copy.176
  419.1 3.6 copy.194
  422.7 2.1 maximum_bitcast_fusion.1
  424.9 3.4 copy.184
  428.2 79.4 %all-to-all-done.3 = bf16[64,16,2048]{2,1,0:T(8,128)(2,1)} async-done(((bf16[64,16,2048]{2,1,0:T(8,128)(2,1)}), bf16[64,16,2048]{2,1,0:T(8,128)(2,1)}, u32[]{:S(2)}, u32[]{:S(2)}) %all-to-all-start.3) | async-done | bytes 4194336 | tf_op jit(solution)/shard_map/all_to_all | solution.py:115
  507.6 3.6 copy.193
  511.2 2.1 maximum_bitcast_fusion
  513.4 3.4 copy.183
  516.7 57.7 %while.3 = (s32[]{:T(128)}, f32[16,128]{1,0:T(8,128)S(1)}, f32[16,128,128]{2,1,0:T(8,128)}, bf16[16,128,128]{1,2,0:T(8,128)(2,1)}, bf16[16,1152,128]{2,1,0:T(8,1...) while((s32[]{:T(128)}, f32[16,128]{1,0:T(8,128)S(1)}, ...), condition=%wide.region_5.7_spmd, body=%wide.region_2.6_spmd.sunk | while | flops 76824320 | bytes 2905185 | solution.py:124
  518.1 1.9 fusion.70
  521.7 1.9 fusion.70
  525.3 1.9 fusion.70
  528.9 1.9 fusion.70
  532.5 1.9 fusion.70
  536.1 1.9 fusion.70
  539.7 1.9 fusion.70
  543.3 1.9 fusion.70
  546.9 1.9 fusion.70
  550.6 1.9 fusion.70
  554.2 1.9 fusion.70
  557.8 1.9 fusion.70
  561.4 1.9 fusion.70
  565.0 1.9 fusion.70
  568.6 1.9 fusion.70
  572.2 1.9 fusion.70
  574.4 2.5 divide_bitcast_fusion
  (140 shorter events, 71.9 us)
Async XLA Ops:
  3.6 79.8 %all-to-all-start = ((bf16[128,64,32]{0,2,1:T(8,128)(2,1)}), bf16[128,64,32]{0,2,1:T(8,128)(2,1)S(1)}, u32[]{:S(2)}, u32[]{:S(2)}) async-start(bf16[128,64,32]{0,2,1:T(8,128)(2,1)} %bitcast.5), calls=%async_computation | async-start | bytes 1048576 | tf_op jit(solution)/shard_map/all_to_all | solution.py:87
  75.3 6.9 %copy-start.7 = (s32[1,64]{1,0:T(1,128)S(1)}, s32[1,64]{1,0:T(1,128)}, u32[]{:S(2)}) copy-start(s32[1,64]{1,0:T(1,128)} %param.25) | copy-start | bytes 772
  83.4 21.3 %copy-start.2 = (bf16[128,64,32]{0,2,1:T(8,128)(2,1)}, bf16[128,64,32]{0,2,1:T(8,128)(2,1)S(1)}, u32[]{:S(2)}) copy-start(bf16[128,64,32]{0,2,1:T(8,128)(2,1)S(1)} %all-to-all-done) | copy-start | bytes 1572868
  83.4 174.6 %all-to-all-start.2 = ((s32[1,64,1]{2,0,1:T(1,128)}), s32[1,64,1]{2,0,1:T(1,128)S(1)}, u32[]{:S(2)}, u32[]{:S(2)}) async-start(s32[1,64,1]{2,0,1:T(1,128)} %copy.178), calls=%async_computation.2 | async-start | bytes 65536 | tf_op jit(solution)/shard_map/all_to_all | solution.py:110
  182.3 0.7 copy-start.1
  200.3 52.4 %copy-start.6 = (f32[128]{0:T(128)S(1)}, f32[128]{0:T(128)}, u32[]{:S(2)}) copy-start(f32[128]{0:T(128)} %iota_add_fusion) | copy-start | bytes 1540
  201.0 53.7 %copy-start.9 = (f32[32]{0:T(128)S(1)}, f32[32]{0:T(128)}, u32[]{:S(2)}) copy-start(f32[32]{0:T(128)} %dynamic_slice.30) | copy-start | bytes 388
  202.1 52.7 %copy-start.3 = (bf16[128,64,32]{0,2,1:T(8,128)(2,1)S(1)}, bf16[128,64,32]{0,2,1:T(8,128)(2,1)}, u32[]{:S(2)}) copy-start(bf16[128,64,32]{0,2,1:T(8,128)(2,1)} %copy-done.2) | copy-start | bytes 1572868
  254.8 17.4 %copy-start = (bf16[128,2048]{1,0:T(8,128)(2,1)S(1)}, bf16[128,2048]{1,0:T(8,128)(2,1)}, u32[]{:S(2)}) copy-start(bf16[128,2048]{1,0:T(8,128)(2,1)} %param.23) | copy-start | bytes 1572868
  258.0 28.0 %all-to-all-start.1 = ((bf16[64,128,32]{1,2,0:T(8,128)(2,1)}), bf16[64,128,32]{1,2,0:T(8,128)(2,1)S(1)}, u32[]{:S(2)}, u32[]{:S(2)}) async-start(bf16[64,128,32]{1,2,0:T(8,128)(2,1)} %copy.175), calls=%async_computation.1 | async-start | bytes 1048576 | tf_op jit(solution)/shard_map/all_to_all | solution.py:95
  272.2 22.6 %copy-start.5 = (f32[2048]{0:T(1024)S(1)}, f32[2048]{0:T(1024)}, u32[]{:S(2)}) copy-start(f32[2048]{0:T(1024)} %param.24) | copy-start | bytes 24580
  405.7 11.9 %copy-start.8 = (s32[1,64]{1,0:T(1,128)S(1)}, s32[1,64]{1,0:T(1,128)}, u32[]{:S(2)}) copy-start(s32[1,64]{1,0:T(1,128)} %param.25) | copy-start | bytes 772
  405.7 101.9 %all-to-all-start.3 = ((bf16[64,16,2048]{2,1,0:T(8,128)(2,1)}), bf16[64,16,2048]{2,1,0:T(8,128)(2,1)}, u32[]{:S(2)}, u32[]{:S(2)}) async-start(bf16[64,16,2048]{2,1,0:T(8,128)(2,1)} %get-tuple-element.125), calls=%async_computation.3 | async-start | bytes 8388608 | tf_op jit(solution)/shard_map/all_to_all | solution.py:115
  419.1 3.7 copy-start.4
where the time goes:
time: 589 us; the launch traced here: 580 us
  local copies, waits for them, and re-layouts  236 us (40%)
  blocking collectives  111 us (19%)
  waiting for transfers between devices  90.5 us (15%)
  matrix products  57.4 us (10%)
  other arithmetic  43.1 us (7%)
  starting transfers between devices  41.1 us (7%)
    all_to_all x1, blocking collectives, local(): lax.all_to_all(send_values, 'seq', split_axis=0, concat_axis=0, tiled=True)  102 us
    pad x8, local copies, waits for them, and re-layouts, modal_group(): states, _ = lax.associative_scan(link_states, (ends, stepped), axis=0)  83.9 us
    all_to_all x1, waiting for transfers between devices, local(): lax.all_to_all(send_keys, 'seq', split_axis=0, concat_axis=0, tiled=True)  79.4 us
    gather x2, local copies, waits for them, and re-layouts, modal_group(): toeplitz = jnp.where(spread[None] >= 0, kernel[:, jnp.clip(spread, 0)], 0.0)  59.9 us
    unnamed x30, local copies, waits for them, and re-layouts  32.9 us
    slice x16, local copies, waits for them, and re-layouts, modal_group(): states, _ = lax.associative_scan(link_states, (ends, stepped), axis=0)  32.1 us
    dot_general x16, matrix products, head_partial(): jnp.dot(weights.astype(jnp.bfloat16), values, preferred_element_type=jnp....  30.6 us
    dot_general x16, matrix products, head_partial(): jnp.einsum('qd,kd->qk', queries, keys, preferred_element_type=jnp.float32)  21.7 us
  transfers between devices with their start and end apart: 4, of which 2 were waited for; matrix products, arithmetic and copies ran while one was open for 43% of the time, Pallas kernels for 0%

commit v1 on v0

v1 whole, which is shorter than its diff:
```python
import functools

import jax
import jax.numpy as jnp
from jax import lax
from jax.experimental import pallas as pl
from jax.experimental.pallas import tpu as pltpu
from jax.sharding import PartitionSpec as P

MESH = pl.DeviceIdType.MESH
LANES = 128
TILE = 16
GROUP = 4
F32 = jnp.float32
BF16 = jnp.bfloat16


def remote(src, dst, send, recv, **where):
    return pltpu.make_async_remote_copy(
        src_ref=src,
        dst_ref=dst,
        send_sem=send,
        recv_sem=recv,
        device_id=where,
        device_id_type=MESH,
    )


def drain(ref, sem):
    pltpu.make_async_copy(ref, ref, sem).wait()


def kernel(
    shards,
    planes,
    modes,
    residual,
    hyena_q,
    hyena_k,
    hyena_v,
    residue_ref,
    rate_ref,
    skip_ref,
    attn_q,
    attn_k,
    gain_ref,
    readers,
    out,
    hk,
    hv,
    hq,
    res,
    decay,
    xs,
    ys,
    ends,
    st_in,
    st_out,
    start,
    stream,
    sq,
    vloc,
    q_all,
    k_all,
    v_all,
    rd_all,
    rd_smem,
    tiles,
    weights,
    totals,
    o_stage,
    o_recv,
    out_v,
    load_sem,
    st_send,
    st_recv,
    back_send,
    back_recv,
    sq_send,
    sq_recv,
    rd_send,
    rd_recv,
    q_send,
    q_recv,
    k_send,
    k_recv,
    v_send,
    v_recv,
    kf_send,
    vf_send,
    o_send,
    o_recv_sem,
    out_sem,
):
    me = lax.axis_index("seq")
    plane = lax.axis_index("chan")
    heads = shards // GROUP
    mine = me // GROUP
    rank = me % GROUP
    core_peer = me + 1 - 2 * (me % 2)
    chip_peer = me + 2 - 4 * ((me // 2) % 2)
    core_rank = core_peer % GROUP
    chip_rank = chip_peer % GROUP
    far_rank = (GROUP - 1) - rank
    rows = hk.shape[0]
    ltiles = hk.shape[1] // LANES

    loads = [
        pltpu.make_async_copy(src, dst, load_sem.at[n])
        for n, (src, dst) in enumerate(
            ((hyena_k, hk), (hyena_v, hv), (hyena_q, hq), (residual, res))
        )
    ]
    for load in loads:
        load.start()

    barrier = pltpu.get_barrier_semaphore()

    @pl.loop(1, shards)
    def _(d):
        pl.semaphore_signal(
            barrier, inc=1, device_id={"seq": (me + d) % shards}, device_id_type=MESH
        )

    for d in range(1, planes):
        pl.semaphore_signal(
            barrier, inc=1, device_id={"chan": (plane + d) % planes}, device_id_type=MESH
        )

    decay[...] = jnp.exp(-rate_ref[...])
    loads[0].wait()
    loads[1].wait()

    @pl.loop(0, ltiles)
    def _(lt):
        cols = pl.ds(pl.multiple_of(lt * LANES, LANES), LANES)
        product = (hk[:, cols].astype(F32) * hv[:, cols].astype(F32)).astype(BF16)
        xs[pl.ds(pl.multiple_of(lt * rows, rows), rows), :] = product.astype(F32)

    halves = ltiles // 8
    for half in range(halves):
        part = slice(half * 8, half * 8 + 8)
        base = half * 8 * rows

        def advance(t, states):
            x = xs[pl.ds(base + t, 8, stride=rows), :]
            return tuple(decay[m, part, :] * states[m] + x for m in range(modes))

        states = lax.fori_loop(
            0, rows, advance, tuple(jnp.zeros((8, LANES), F32) for _ in range(modes)), unroll=4
        )
        for m in range(modes):
            slot = (m * ltiles + half * 8) // 4
            ends[slot] = states[m][0:4]
            ends[slot + 1] = states[m][4:8]

    pl.semaphore_wait(barrier, shards - 1 + planes - 1)

    @pl.loop(1, shards)
    def _(d):
        to = (me + d) % shards
        remote(ends.at[to], st_in.at[me], st_send, st_recv, seq=to).start()

    st_in[me] = ends[me]
    blocks_per_mode = ltiles // 4
    my_mode = me // blocks_per_mode
    my_rows = me % blocks_per_mode

    own_cols = pl.ds(pl.multiple_of(mine * LANES, LANES), LANES)
    own_q = pltpu.make_async_copy(attn_q.at[:, :, own_cols], q_all.at[mine], load_sem.at[4])
    own_k = pltpu.make_async_copy(attn_k.at[:, :, own_cols], k_all.at[me], load_sem.at[5])
    own_r = pltpu.make_async_copy(readers, rd_all.at[mine], load_sem.at[6])
    own_q.start()
    own_k.start()
    own_r.start()

    drain(st_in.at[pl.ds(0, shards - 1)], st_recv)
    rate_rows = rate_ref[my_mode, pl.ds(my_rows * 4, 4), :]
    across = jnp.exp(-float(rows) * rate_rows)

    def scan(j, carry):
        st_out[j] = carry
        return across * carry + st_in[j]

    lax.fori_loop(0, shards, scan, jnp.zeros((4, LANES), F32), unroll=4)

    @pl.loop(1, shards)
    def _(d):
        to = (me + d) % shards
        remote(st_out.at[to], start.at[me], back_send, back_recv, seq=to).start()

    start[me] = st_out[me]

    @pl.loop(1, heads)
    def _(d):
        h = (mine + d) % heads
        cols = pl.ds(pl.multiple_of(h * LANES, LANES), LANES)
        to = h * GROUP + rank
        remote(attn_k.at[:, :, cols], k_all.at[me], k_send, k_recv.at[me], seq=to).start()

    @pl.loop(1, heads)
    def _(d):
        h = (mine + d) % heads
        cols = pl.ds(pl.multiple_of(h * LANES, LANES), LANES)
        to = h * GROUP + rank
        remote(attn_q.at[:, :, cols], q_all.at[mine], q_send, q_recv, seq=to).start()
        remote(readers, rd_all.at[mine], rd_send, rd_recv, seq=to).start()

    loads[2].wait()
    loads[3].wait()
    drain(start.at[pl.ds(0, shards - 1)], back_recv)

    for half in range(halves):
        part = slice(half * 8, half * 8 + 8)
        base = half * 8 * rows
        first = []
        for m in range(modes):
            slot = (m * ltiles + half * 8) // 4
            first.append(jnp.concatenate([start[slot], start[slot + 1]], axis=0))
        skip = skip_ref[part, :]

        def filtered(t, states):
            x = xs[pl.ds(base + t, 8, stride=rows), :]
            states = tuple(decay[m, part, :] * states[m] + x for m in range(modes))
            terms = [residue_ref[m, part, :] * states[m] for m in range(modes)]
            terms.append(skip * x)
            while len(terms) > 1:
                paired = [terms[n] + terms[n + 1] for n in range(0, len(terms) - 1, 2)]
                terms = paired + terms[len(paired) * 2 :]
            ys[pl.ds(base + t, 8, stride=rows), :] = terms[0]
            return states

        lax.fori_loop(0, rows, filtered, tuple(first), unroll=4)

    def streamed(lt, acc):
        cols = pl.ds(pl.multiple_of(lt * LANES, LANES), LANES)
        convolved = ys[pl.ds(pl.multiple_of(lt * rows, rows), rows), :].astype(BF16).astype(F32)
        value = res[:, cols].astype(F32) + hq[:, cols].astype(F32) * convolved
        stream[lt] = value
        return acc + value * value

    acc = lax.fori_loop(0, ltiles, streamed, jnp.zeros((rows, LANES), F32))
    sq[plane] = lax.dot_general(
        jnp.ones((8, LANES), F32),
        acc,
        (((1,), (1,)), ((), ())),
        precision=lax.Precision.HIGHEST,
        preferred_element_type=F32,
    )
    for d in range(1, planes):
        to = (plane + d) % planes
        remote(sq.at[plane], sq.at[plane], sq_send, sq_recv, chan=to).start()
    drain(sq.at[pl.ds(0, planes - 1)], sq_recv)
    total_sq = sq[0]
    for n in range(1, planes):
        total_sq = total_sq + sq[n]
    width = float(planes * ltiles * LANES)
    scale = lax.rsqrt(total_sq / width + 1e-6).T[:, 0:1]

    def normed(h):
        value = stream[h] * scale * gain_ref[pl.ds(h, 1), :]
        return value.astype(BF16).reshape(rows // TILE, TILE, LANES)

    @pl.loop(1, heads)
    def _(d):
        h = (mine + d) % heads
        vloc[h] = normed(h)
        to = h * GROUP + rank
        remote(vloc.at[h], v_all.at[me], v_send, v_recv.at[me], seq=to).start()

    v_all[me] = normed(mine)

    def share(everything, recv, fwd):
        def pass_on(slot, to):
            remote(everything.at[slot], everything.at[slot], fwd, recv.at[slot], seq=to).start()

        pass_on(me, core_peer)
        pass_on(me, chip_peer)

        @pl.loop(1, heads)
        def _(d):
            slot = ((mine + heads - d) % heads) * GROUP + rank
            drain(everything.at[slot], recv.at[slot])
            pass_on(slot, core_peer)
            pass_on(slot, chip_peer)

        @pl.loop(0, heads)
        def _(d):
            slot = ((mine + heads - d) % heads) * GROUP + chip_rank
            drain(everything.at[slot], recv.at[slot])
            pass_on(slot, core_peer)

        @pl.loop(0, heads)
        def _(n):
            slot = n * GROUP + core_rank
            drain(everything.at[slot], recv.at[slot])
            slot = n * GROUP + far_rank
            drain(everything.at[slot], recv.at[slot])

    own_k.wait()
    share(k_all, k_recv, kf_send)

    own_q.wait()
    own_r.wait()
    drain(q_all.at[pl.ds(0, heads - 1)], q_recv)
    drain(rd_all.at[pl.ds(0, heads - 1)], rd_recv)
    to_smem = pltpu.make_async_copy(rd_all, rd_smem, load_sem.at[7])
    to_smem.start()
    to_smem.wait()

    def pick(everything, i):
        for j in range(shards):
            tiles[j * TILE : (j + 1) * TILE, :] = everything[j, rd_smem[i, 0, shards + j]]

    remote_keys = shards * TILE
    root = 1.0 / float(LANES) ** 0.5
    across_lanes = (((1,), (1,)), ((), ()))

    @pl.loop(0, heads)
    def _(i):
        query = q_all[i].reshape(rows, LANES)
        pick(k_all, i)
        lane_tile = lax.broadcasted_iota(jnp.int32, (1, LANES), 1) // TILE
        row = lax.broadcasted_iota(jnp.int32, (rows, rows), 0)
        col = lax.broadcasted_iota(jnp.int32, (rows, rows), 1)
        own = lax.dot_general(
            query, k_all[i * GROUP + rank].reshape(rows, LANES), across_lanes, preferred_element_type=F32
        )
        own = jnp.where(row >= col, own * root, -1e30)
        far = lax.dot_general(query, tiles[...], across_lanes, preferred_element_type=F32)
        masked = []
        per = LANES // TILE
        for c in range(remote_keys // LANES):
            wanted = jnp.full((1, LANES), -1, jnp.int32)
            for n in range(per):
                wanted = jnp.where(lane_tile == n, rd_smem[i, 0, c * per + n], wanted)
            masked.append(
                jnp.where(wanted >= 0, far[:, c * LANES : (c + 1) * LANES] * root, -1e30)
            )
        peak = own
        for block in masked:
            peak = jnp.maximum(peak, block)
        peak = jnp.max(peak, axis=1, keepdims=True)
        own = jnp.exp(own - peak)
        total = own
        weights[i, :, remote_keys:] = own.astype(BF16)
        for c, block in enumerate(masked):
            block = jnp.exp(block - peak)
            total = total + block
            weights[i, :, c * LANES : (c + 1) * LANES] = block.astype(BF16)
        total = jnp.sum(total, axis=1, keepdims=True)
        totals[i] = jnp.broadcast_to(1.0 / total, (rows, LANES))

    share(v_all, v_recv, vf_send)

    def attend(i):
        pick(v_all, i)
        summed = jnp.dot(weights[i, :, 0:remote_keys], tiles[...], preferred_element_type=F32)
        summed += jnp.dot(
            weights[i, :, remote_keys:],
            v_all[i * GROUP + rank].reshape(rows, LANES),
            preferred_element_type=F32,
        )
        return (summed * totals[i]).astype(BF16)

    @pl.loop(1, heads)
    def _(d):
        i = (mine + d) % heads
        o_stage[i] = attend(i)
        remote(
            o_stage.at[i], o_recv.at[mine], o_send, o_recv_sem.at[mine], seq=i * GROUP + rank
        ).start()

    o_recv[mine] = attend(mine)

    def finish(h):
        cols = pl.ds(pl.multiple_of(h * LANES, LANES), LANES)
        out_v[:, cols] = (stream[h] + o_recv[h].astype(F32)).astype(BF16)

    finish(mine)

    @pl.loop(1, heads)
    def _(d):
        h = (mine + heads - d) % heads
        drain(o_recv.at[h], o_recv_sem.at[h])
        finish(h)

    written = pltpu.make_async_copy(out_v, out, out_sem)
    written.start()

    drain(ends.at[pl.ds(0, shards - 1)], st_send)
    drain(st_out.at[pl.ds(0, shards - 1)], back_send)
    drain(sq.at[pl.ds(0, planes - 1)], sq_send)
    drain(rd_all.at[pl.ds(0, heads - 1)], rd_send)
    drain(q_all.at[pl.ds(0, heads - 1)], q_send)
    drain(q_all.at[pl.ds(0, heads - 1)], k_send)
    drain(q_all.at[pl.ds(0, heads - 1)], v_send)
    drain(q_all.at[pl.ds(0, heads - 1)], o_send)
    drain(k_all.at[pl.ds(0, 3 * heads)], kf_send)
    drain(v_all.at[pl.ds(0, 3 * heads)], vf_send)
    written.wait()


def local(
    shards,
    planes,
    residual,
    hyena_q,
    hyena_k,
    hyena_v,
    modal_residue,
    decay_rate,
    skip_gain,
    attn_q,
    attn_k,
    norm_gain,
    readers,
):
    rows, features = residual.shape
    modes = modal_residue.shape[1]
    ltiles = features // LANES
    heads = shards // GROUP

    def modal(array):
        return array.T.reshape(modes, ltiles, LANES)

    hbm = pl.BlockSpec(memory_space=pl.ANY)
    vmem = pl.BlockSpec(memory_space=pltpu.VMEM)
    dma = pltpu.SemaphoreType.DMA
    wanted = jnp.concatenate([readers, jnp.clip(readers, 0)], axis=1)
    tiled = (rows // TILE, TILE, features)
    block = (rows // TILE, TILE, LANES)
    return pl.pallas_call(
        functools.partial(kernel, shards, planes, modes),
        out_shape=jax.ShapeDtypeStruct((rows, features), BF16),
        in_specs=[hbm, hbm, hbm, hbm, vmem, vmem, vmem, hbm, hbm, vmem, hbm],
        out_specs=hbm,
        scratch_shapes=[
            pltpu.VMEM((rows, features), BF16),
            pltpu.VMEM((rows, features), BF16),
            pltpu.VMEM((rows, features), BF16),
            pltpu.VMEM((rows, features), BF16),
            pltpu.VMEM((modes, ltiles, LANES), F32),
            pltpu.VMEM((ltiles * rows, LANES), F32),
            pltpu.VMEM((ltiles * rows, LANES), F32),
            pltpu.VMEM((shards, 4, LANES), F32),
            pltpu.VMEM((shards, 4, LANES), F32),
            pltpu.VMEM((shards, 4, LANES), F32),
            pltpu.VMEM((shards, 4, LANES), F32),
            pltpu.VMEM((ltiles, rows, LANES), F32),
            pltpu.VMEM((planes, 8, LANES), F32),
            pltpu.VMEM((heads,) + block, BF16),
            pltpu.VMEM((heads,) + block, BF16),
            pltpu.VMEM((shards,) + block, BF16),
            pltpu.VMEM((shards,) + block, BF16),
            pltpu.VMEM((heads, 1, LANES), jnp.int32),
            pltpu.SMEM((heads, 1, LANES), jnp.int32),
            pltpu.VMEM((shards * TILE, LANES), BF16),
            pltpu.VMEM((heads, rows, shards * TILE + rows), BF16),
            pltpu.VMEM((heads, rows, LANES), F32),
            pltpu.VMEM((heads, rows, LANES), BF16),
            pltpu.VMEM((heads, rows, LANES), BF16),
            pltpu.VMEM((rows, features), BF16),
            dma((8,)),
            dma,
            dma,
            dma,
            dma,
            dma,
            dma,
            dma,
            dma,
            dma,
            dma,
            dma,
            dma((shards,)),
            dma,
            dma((shards,)),
            dma,
            dma,
            dma,
            dma((heads,)),
            dma,
        ],
        compiler_params=pltpu.CompilerParams(
            collective_id=0, has_side_effects=True, vmem_limit_bytes=48 * 1024 * 1024
        ),
    )(
        residual,
        hyena_q,
        hyena_k,
        hyena_v,
        modal(modal_residue),
        modal(decay_rate),
        skip_gain.reshape(ltiles, LANES),
        attn_q.reshape(tiled),
        attn_k.reshape(tiled),
        norm_gain.reshape(ltiles, LANES),
        wanted,
    )


def solution(mesh):
    spread = P("seq", "chan")
    placed = (
        spread,
        spread,
        spread,
        spread,
        P("chan", None),
        P("chan", None),
        P("chan"),
        spread,
        spread,
        P("chan"),
        P("seq", None),
    )
    return jax.shard_map(
        functools.partial(local, mesh.shape["seq"], mesh.shape["chan"]),
        mesh=mesh,
        in_specs=placed,
        out_specs=spread,
        check_vma=False,
    )
```

time: 589 us -> 109 us (0.19); the launches traced: 580 us -> 109 us
  local copies, waits for them, and re-layouts: 236 us -> 7.88 us
  blocking collectives: 111 us -> 0 us
  Pallas kernels: 0 us -> 99.4 us
  waiting for transfers between devices: 90.5 us -> 0 us
  matrix products: 57.4 us -> 0 us
  other arithmetic: 43.1 us -> 1.44 us
  starting transfers between devices: 41.1 us -> 0 us
    all_to_all x1 -> x0, blocking collectives: 102 us -> none  [local(): lax.all_to_all(send_values, 'seq', split_axis=0, concat_axis=0, tiled=True)]
    pallas_call x0 -> x1, Pallas kernels: none -> 99.4 us  [local(): pl.pallas_call(functools.partial(kernel, shards, planes, modes), out_shap...]
    all_to_all x4 -> x0, waiting for transfers between devices: 90.5 us -> none  [the longest x1 79.4 us: local(): lax.all_to_all(send_keys, 'seq', split_axis=0, concat_axis=0, tiled=True)]
    pad x8 -> x0, local copies, waits for them, and re-layouts: 83.9 us -> none  [modal_group(): states, _ = lax.associative_scan(link_states, (ends, stepped), axis=0)]
    gather x4 -> x0, local copies, waits for them, and re-layouts: 65.5 us -> none  [the longest x2 59.9 us: modal_group(): toeplitz = jnp.where(spread[None] >= 0, kernel[:, jnp.clip(spread, 0)], 0.0)]
    dot_general x35 -> x0, matrix products: 57.4 us -> none  [the longest x16 30.6 us: head_partial(): jnp.dot(weights.astype(jnp.bfloat16), values, preferred_element_type=jnp....]
    all_to_all x4 -> x0, starting transfers between devices: 41.1 us -> none  [the longest x1 13.2 us: local(): lax.all_to_all(product, 'seq', split_axis=1, concat_axis=0, tiled=True)]
    slice x17 -> x0, local copies, waits for them, and re-layouts: 36.6 us -> none  [the longest x16 32.1 us: modal_group(): states, _ = lax.associative_scan(link_states, (ends, stepped), axis=0)]
  transfers between devices with their start and end apart: 4 -> 0, of which waited for: 2 -> 0; matrix products, arithmetic and copies ran while one was open for 43% -> 0% of each run, Pallas kernels for 0% -> 0%
where the time goes in v1:
time: 109 us
  Pallas kernels  99.4 us (91%)
  local copies, waits for them, and re-layouts  7.88 us (7%)
  other arithmetic  1.44 us (1%)
    pallas_call x1, Pallas kernels, local(): pl.pallas_call(functools.partial(kernel, shards, planes, modes), out_shap...  99.4 us
    unnamed x19, local copies, waits for them, and re-layouts  7.88 us

profile of v1, /device:TPU:1, one launch (start us, length us, event | category | flops | bytes accessed | tf_op | source)
XLA Modules:
  0.0 108.8 jit_solution(8894802632431857364)
XLA Ops:
  0.0 0.0 copy-start
  0.0 0.7 broadcast_maximum_fusion
  0.7 0.7 pad_add_fusion.readers
  1.4 0.9 copy.12
  2.4 0.0 copy-start.6
  2.4 0.0 copy-start.7
  2.4 0.9 copy.13
  3.3 0.0 copy-done
  3.4 0.0 copy-done.6
  3.4 0.0 copy-done.7
  3.4 0.0 copy-start.1
  3.4 1.0 copy-done.1
  4.4 0.0 copy-start.2
  4.4 1.0 copy-done.2
  5.5 0.0 copy-start.3
  5.5 1.0 copy-done.3
  6.5 0.0 copy-start.4
  6.5 1.0 copy-done.4
  7.5 0.0 copy-start.5
  7.6 1.0 copy-done.5
  8.6 99.4 %shard_map.109 = bf16[128,2048]{1,0:T(8,128)(2,1)S(1)} custom-call(bf16[128,2048]{1,0:T(8,128)(2,1)S(1)} %copy-done, bf16[128,2048]{1,0:T(8,128)(2,1)S(1)} %copy-done.1, bf16[128,2048]{1,0:T(8,128)(2,1)S(1)} %copy-done.2, bf16[128,2048]{1,0:T(8,128)(2,1)S(1)} %copy-done.3, f32[16,16,128]{2,1,0:T(8,128)S(1)} %bitcast.12, f32[16,16,128]{2,1,0:T(8,128)S(1)} %bitcast.13, ...), custom_call_target="tpu_custom_call" | custom-call | tf_op jit(solution)/shard_map/pallas_call | solution.py:433
  108.0 0.8 copy.15
Async XLA Ops:
  0.0 3.3 %copy-start = (bf16[128,2048]{1,0:T(8,128)(2,1)S(1)}, bf16[128,2048]{1,0:T(8,128)(2,1)}, u32[]{:S(2)}) copy-start(bf16[128,2048]{1,0:T(8,128)(2,1)} %residual.1) | copy-start | bytes 1572868
  2.4 1.0 copy-start.6
  2.4 1.0 copy-start.7
  3.4 1.0 copy-start.1
  4.4 1.0 copy-start.2
  5.5 1.0 copy-start.3
  6.5 1.0 copy-start.4
  7.5 1.0 copy-start.5

commit v2 on v1

v2 whole, which is shorter than its diff:
```python
import functools

import jax
import jax.numpy as jnp
from jax import lax
from jax.experimental import pallas as pl
from jax.experimental.pallas import tpu as pltpu
from jax.sharding import PartitionSpec as P

MESH = pl.DeviceIdType.MESH
LANES = 128
TILE = 16
GROUP = 4
LEVEL = 8
SHARE_LAG = 5
BLOCKS_AT = (3, 1, 3, 3, 6)
F32 = jnp.float32
BF16 = jnp.bfloat16


def remote(src, dst, send, recv, **where):
    return pltpu.make_async_remote_copy(
        src_ref=src,
        dst_ref=dst,
        send_sem=send,
        recv_sem=recv,
        device_id=where,
        device_id_type=MESH,
    )


def drain(ref, sem):
    pltpu.make_async_copy(ref, ref, sem).wait()


def kernel(
    shards,
    planes,
    modes,
    residual,
    hyena_q,
    hyena_k,
    hyena_v,
    residue_hbm,
    rate_hbm,
    skip_hbm,
    attn_q,
    attn_k,
    gain_hbm,
    readers_hbm,
    out,
    residue_ref,
    rate_ref,
    skip_ref,
    gain_ref,
    readers,
    hk,
    hv,
    hq,
    res,
    by_tile,
    rates,
    residues,
    decay,
    xs,
    ys,
    ends,
    st_in,
    level,
    level_in,
    st_out,
    start,
    stream,
    sq,
    vloc,
    q_all,
    k_all,
    v_all,
    rd_mine,
    rd_all,
    rd_smem,
    tiles,
    weights,
    totals,
    o_stage,
    o_recv,
    out_v,
    load_sem,
    own_sem,
    st_send,
    st_recv,
    level_send,
    level_recv,
    back_send,
    back_recv,
    sq_send,
    sq_recv,
    rd_send,
    rd_recv,
    q_send,
    q_recv,
    k_send,
    k_recv,
    v_send,
    v_recv,
    kf_send,
    vf_send,
    o_send,
    o_recv_sem,
    out_sem,
):
    me = lax.axis_index("seq")
    plane = lax.axis_index("chan")
    heads = shards // GROUP
    mine = me // GROUP
    core = me % 2
    side = (me // 2) % 2
    core_peer = me + 1 - 2 * core
    chip_peer = me + 2 - 4 * side
    middle = shards // 2
    half = me // middle
    turned = (mine // 2) % 2
    my_half = (side + turned) % 2
    my_row = (me % middle) // 2
    place = me % LEVEL
    level_at = me // LEVEL
    levels = shards // LEVEL
    rows = hk.shape[0]
    ltiles = hk.shape[1] // LANES

    loads = [
        pltpu.make_async_copy(src, dst, load_sem.at[n])
        for n, (src, dst) in enumerate(
            (
                (hyena_k, hk),
                (hyena_v, hv),
                (rate_hbm, rate_ref),
                (residue_hbm, residue_ref),
                (readers_hbm, readers),
                (skip_hbm, skip_ref),
                (gain_hbm, gain_ref),
                (hyena_q, hq),
                (residual, res),
            )
        )
    ]
    for load in loads:
        load.start()

    barrier = pltpu.get_barrier_semaphore()

    @pl.loop(0, LEVEL // 2)
    def _(n):
        to = level_at * LEVEL + 2 * n + 1 - core
        pl.semaphore_signal(barrier, inc=1, device_id={"seq": to}, device_id_type=MESH)

    for d in range(1, planes):
        to = (plane + d) % planes
        pl.semaphore_signal(barrier, inc=1, device_id={"chan": to}, device_id_type=MESH)

    @pl.loop(1, middle)
    def _(d):
        to = (me + 2 * d) % shards
        pl.semaphore_signal(barrier, inc=1, device_id={"seq": to}, device_id_type=MESH)

    def order(n):
        return heads // 2 + (1 - n % 2) * (n // 2) - (n % 2) * ((n + 1) // 2)

    def columns(h):
        return pl.ds(pl.multiple_of(h * LANES, LANES), LANES)

    def reader_of(h):
        return h * GROUP + 2 * ((half + h // 2) % 2) + core

    def holder_of(h):
        return h * GROUP + 2 * (half * ((1 + h // 2) % 2) + (1 - half) * side) + core

    at_home = half == my_half
    held_here = jnp.logical_or(half == 0, at_home)

    def send_keys(low, high):
        @pl.loop(low, high)
        def _(n):
            send_key(n)

    def send_key(n):
        h = (mine + order(n)) % heads
        remote(
            attn_k.at[:, :, columns(h)], k_all.at[me], k_send, k_recv.at[me], seq=holder_of(h)
        ).start()

    def send_query(n):
        h = (mine + order(n)) % heads
        to = reader_of(h)
        remote(rd_mine, rd_all.at[my_row], rd_send, rd_recv.at[my_row], seq=to).start()
        remote(
            attn_q.at[:, :, columns(h)], q_all.at[my_row], q_send, q_recv.at[my_row], seq=to
        ).start()

    def send_queries(low, high):
        @pl.loop(low, high)
        def _(n):
            send_query(n)

    def send_blocks(low, high):
        split = heads - 1
        if low < min(high, split):
            send_keys(low, min(high, split))
        if max(low, split) < high:
            send_queries(max(low, split) - split, high - split)

    def keep_key():
        @pl.when(held_here)
        def _():
            pltpu.make_async_copy(
                attn_k.at[:, :, columns(mine)], k_all.at[me], k_recv.at[me]
            ).start()

        @pl.when(jnp.logical_not(held_here))
        def _():
            remote(
                attn_k.at[:, :, columns(mine)],
                k_all.at[me],
                own_sem.at[0],
                k_recv.at[me],
                seq=chip_peer,
            ).start()

    def keep_query():
        @pl.when(at_home)
        def _():
            pltpu.make_async_copy(
                attn_q.at[:, :, columns(mine)], q_all.at[my_row], q_recv.at[my_row]
            ).start()
            pltpu.make_async_copy(rd_mine, rd_all.at[my_row], rd_recv.at[my_row]).start()

        @pl.when(jnp.logical_not(at_home))
        def _():
            remote(
                attn_q.at[:, :, columns(mine)],
                q_all.at[my_row],
                own_sem.at[1],
                q_recv.at[my_row],
                seq=chip_peer,
            ).start()
            remote(
                rd_mine, rd_all.at[my_row], own_sem.at[2], rd_recv.at[my_row], seq=chip_peer
            ).start()

    pl.semaphore_wait(barrier, LEVEL // 2 + planes - 1 + middle - 1)
    at_entry, at_stretch, at_share, at_level, at_back = BLOCKS_AT
    send_blocks(0, at_entry)
    issued = at_entry

    loads[2].wait()
    loads[3].wait()
    loads[4].wait()

    def spread_modes(lt, _):
        cols = pl.ds(pl.multiple_of(lt * LANES, LANES), LANES)
        at = pl.ds(pl.multiple_of(lt * modes, modes), modes)
        by_tile[0, at, :] = rate_ref[:, cols]
        by_tile[1, at, :] = residue_ref[:, cols]
        return _

    lax.fori_loop(0, ltiles, spread_modes, 0)
    for m in range(modes):
        for part in range(ltiles // 8):
            of_mode = pl.ds(part * 8 * modes + m, 8, stride=modes)
            sub = slice(m * ltiles + part * 8, m * ltiles + part * 8 + 8)
            rate = by_tile[0, of_mode, :]
            rates[sub, :] = rate
            decay[sub, :] = jnp.exp(-rate)
            residues[sub, :] = by_tile[1, of_mode, :]
    wanted = readers[...]
    rd_mine[...] = jnp.zeros_like(rd_mine)
    rd_mine[0:1, 0:shards] = wanted
    rd_mine[1:2, 0:shards] = jnp.maximum(wanted, 0)
    loads[0].wait()
    loads[1].wait()

    @pl.loop(0, ltiles)
    def _(lt):
        cols = pl.ds(pl.multiple_of(lt * LANES, LANES), LANES)
        product = (hk[:, cols].astype(F32) * hv[:, cols].astype(F32)).astype(BF16)
        xs[pl.ds(pl.multiple_of(lt * rows, rows), rows), :] = product.astype(F32)

    per_place = modes // LEVEL
    parts = ltiles // 8

    def mode_rows(m, part):
        return slice(m * ltiles + part * 8, m * ltiles + part * 8 + 8)

    def share_rows(m, part):
        at = (m % per_place) * ltiles + part * 8
        return slice(at, at + 8)

    for part in range(parts):
        base = part * 8 * rows

        def advance(t, states):
            x = xs[pl.ds(base + t, 8, stride=rows), :]
            return tuple(decay[mode_rows(m, part), :] * states[m] + x for m in range(modes))

        def stretch(n, states, part=part, advance=advance):
            if at_stretch:
                send_key(at_entry + part * 2 + n)
            span = rows // 2

            def inner(t, states):
                return advance(n * span + t, states)

            return lax.fori_loop(0, span, inner, states, unroll=4)

        states = lax.fori_loop(
            0, 2, stretch, tuple(jnp.zeros((8, LANES), F32) for _ in range(modes))
        )
        for m in range(modes):
            ends[m // per_place, share_rows(m, part), :] = states[m]

    issued += 2 * parts * at_stretch

    @pl.loop(1, LEVEL)
    def _(d):
        at = (place + d) % LEVEL
        to = level_at * LEVEL + at
        remote(ends.at[at], st_in.at[place], st_send, st_recv, seq=to).start()

    st_in[place] = ends[place]
    send_blocks(issued, issued + at_share)
    issued += at_share

    my_rates = rates[pl.ds(pl.multiple_of(place * per_place * ltiles, 8), per_place * ltiles), :]
    across = jnp.exp(-float(rows) * my_rates)
    across_level = jnp.exp(-float(rows * LEVEL) * my_rates)
    drain(st_in.at[pl.ds(0, LEVEL - 1)], st_recv)
    carry = st_in[0]
    for n in range(1, LEVEL):
        carry = across * carry + st_in[n]
    level[...] = carry

    @pl.loop(level_at + 1, levels)
    def _(to):
        remote(
            level,
            level_in.at[level_at],
            level_send.at[to],
            level_recv.at[level_at],
            seq=to * LEVEL + place,
        ).start()

    send_blocks(issued, issued + at_level)
    issued += at_level

    def before(n, carry):
        drain(level_in.at[n], level_recv.at[n])
        return across_level * carry + level_in[n]

    carry = lax.fori_loop(0, level_at, before, jnp.zeros_like(carry))
    for n in range(LEVEL):
        st_out[n] = carry
        carry = across * carry + st_in[n]

    @pl.loop(1, LEVEL)
    def _(d):
        at = (place + d) % LEVEL
        to = level_at * LEVEL + at
        remote(st_out.at[at], start.at[place], back_send, back_recv, seq=to).start()

    start[place] = st_out[place]
    send_blocks(issued, issued + at_back)
    issued += at_back
    keep_key()
    loads[5].wait()
    loads[6].wait()
    loads[7].wait()
    loads[8].wait()
    drain(start.at[pl.ds(0, LEVEL - 1)], back_recv)

    for part in range(parts):
        base = part * 8 * rows
        skip = skip_ref[part * 8 : part * 8 + 8, :]

        def filtered(t, states):
            x = xs[pl.ds(base + t, 8, stride=rows), :]
            states = tuple(decay[mode_rows(m, part), :] * states[m] + x for m in range(modes))
            terms = [residues[mode_rows(m, part), :] * states[m] for m in range(modes)]
            terms.append(skip * x)
            while len(terms) > 1:
                paired = [terms[n] + terms[n + 1] for n in range(0, len(terms) - 1, 2)]
                terms = paired + terms[len(paired) * 2 :]
            ys[pl.ds(base + t, 8, stride=rows), :] = terms[0]
            return states

        first = tuple(start[m // per_place, share_rows(m, part), :] for m in range(modes))

        lax.fori_loop(0, rows, filtered, first, unroll=4)

    def streamed(lt, acc):
        cols = columns(lt)
        convolved = ys[pl.ds(pl.multiple_of(lt * rows, rows), rows), :].astype(BF16).astype(F32)
        value = res[:, cols].astype(F32) + hq[:, cols].astype(F32) * convolved
        stream[lt] = value
        return acc + value * value

    acc = lax.fori_loop(0, ltiles, streamed, jnp.zeros((rows, LANES), F32))
    sq[plane] = lax.dot_general(
        jnp.ones((8, LANES), F32),
        acc,
        (((1,), (1,)), ((), ())),
        precision=lax.Precision.HIGHEST,
        preferred_element_type=F32,
    )
    for d in range(1, planes):
        to = (plane + d) % planes
        remote(sq.at[plane], sq.at[plane], sq_send, sq_recv, chan=to).start()
    send_blocks(issued, 2 * (heads - 1))
    keep_query()

    early = heads // 2

    def sharing(everything, recv, fwd):
        def pass_on(slot, to):
            remote(everything.at[slot], everything.at[slot], fwd, recv.at[slot], seq=to).start()

        def share_slot(slot, to_chip):
            drain(everything.at[slot], recv.at[slot])
            if to_chip:
                pass_on(slot, chip_peer)
            pass_on(slot, core_peer)

        def share_far(n):
            slot = n * GROUP + 2 * (1 - side) + core
            share_slot(slot, False)

        def share_from(n):
            group = (mine + heads - order(n)) % heads

            @pl.when(group < early)
            def _():
                share_slot(group * GROUP + 2 * side + core, True)

            @pl.when(jnp.logical_and(group >= early, my_half == 1))
            def _():
                share_slot(group * GROUP + core, False)
                share_slot(group * GROUP + 2 + core, False)

        def arrive():
            @pl.loop(0, middle // 2)
            def _(n):
                slot = 2 * n + 1 - core
                drain(everything.at[slot], recv.at[slot])

            @pl.when(my_half == 1)
            def _():
                @pl.loop(middle // 2, middle)
                def _(n):
                    slot = 2 * n + 1 - core
                    drain(everything.at[slot], recv.at[slot])

        return share_from, share_far, arrive

    key_from, far_key, keys_arrive = sharing(k_all, k_recv, kf_send)
    pl.loop(0, heads)(key_from)

    def far_keys():
        pl.loop(0, early)(far_key)

    drain(sq.at[pl.ds(0, planes - 1)], sq_recv)
    total_sq = sq[0]
    for n in range(1, planes):
        total_sq = total_sq + sq[n]
    width = float(planes * ltiles * LANES)
    scale = lax.rsqrt(total_sq / width + 1e-6).T[:, 0:1]

    def normed(h):
        value = stream[h] * scale * gain_ref[pl.ds(h, 1), :]
        return value.astype(BF16).reshape(rows // TILE, TILE, LANES)

    @pl.loop(0, heads - 1)
    def _(n):
        h = (mine + order(n)) % heads
        vloc[h] = normed(h)
        remote(vloc.at[h], v_all.at[me], v_send, v_recv.at[me], seq=holder_of(h)).start()

    vloc[mine] = normed(mine)

    @pl.when(held_here)
    def _():
        pltpu.make_async_copy(vloc.at[mine], v_all.at[me], v_recv.at[me]).start()

    @pl.when(jnp.logical_not(held_here))
    def _():
        remote(
            vloc.at[mine], v_all.at[me], own_sem.at[3], v_recv.at[me], seq=chip_peer
        ).start()

    far_keys()
    keys_arrive()

    @pl.loop(0, heads)
    def _(n):
        drain(rd_all.at[n], rd_recv.at[n])

    to_smem = pltpu.make_async_copy(rd_all, rd_smem, load_sem.at[9])
    to_smem.start()
    to_smem.wait()

    def pick(everything, i, count):
        for j in range(count):
            tiles[j * TILE : (j + 1) * TILE, :] = everything[j, rd_smem[i, 1, j]]

    root = 1.4426950408889634 / float(LANES) ** 0.5
    lanes = (((1,), (1,)), ((), ()))

    def weigh(i, count):
        keys = count * TILE
        query = q_all[i].reshape(rows, LANES)
        shard = my_half * middle + 2 * i + core
        pick(k_all, i, count)
        lane_tile = lax.broadcasted_iota(jnp.int32, (1, LANES), 1) // TILE
        row = lax.broadcasted_iota(jnp.int32, (rows, rows), 0)
        col = lax.broadcasted_iota(jnp.int32, (rows, rows), 1)
        own = lax.dot_general(
            query, k_all[shard].reshape(rows, LANES), lanes, preferred_element_type=F32
        )
        far = lax.dot_general(query, tiles[0:keys, :], lanes, preferred_element_type=F32)
        blocks = [jnp.where(row >= col, own * root, -1e30)]
        zero = jnp.zeros((1, LANES), F32)
        per = LANES // TILE
        for c in range(keys // LANES):
            wanted = jnp.full((1, LANES), -1, jnp.int32)
            for n in range(per):
                wanted = jnp.where(lane_tile == n, rd_smem[i, 0, c * per + n], wanted)
            block = far[:, c * LANES : (c + 1) * LANES] * root
            blocks.append(block + jnp.where(wanted >= 0, zero, -1e30))
        peak = blocks[0]
        for block in blocks[1:]:
            peak = jnp.maximum(peak, block)
        peak = jnp.max(peak, axis=1, keepdims=True)
        total = jnp.zeros((rows, LANES), F32)
        for c, block in enumerate(blocks):
            block = jnp.exp2(block - peak)
            total = total + block
            weights[i, :, c * LANES : (c + 1) * LANES] = block.astype(BF16)
        total = jnp.sum(total, axis=1, keepdims=True)
        totals[i] = jnp.broadcast_to(1.0 / total, (rows, LANES))

    share_from, share_far, arrive = sharing(v_all, v_recv, vf_send)

    @pl.loop(0, heads)
    def _(n):
        drain(q_all.at[n], q_recv.at[n])

        @pl.when(n >= SHARE_LAG)
        def _():
            share_from(n - SHARE_LAG)

        @pl.when(my_half == 0)
        def _():
            weigh(n, middle)

        @pl.when(my_half == 1)
        def _():
            weigh(n, shards)

    @pl.loop(heads - SHARE_LAG, heads)
    def _(n):
        share_from(n)

    pl.loop(0, early)(share_far)
    arrive()

    def attend(i, count):
        keys = count * TILE
        pick(v_all, i, count)
        shard = my_half * middle + 2 * i + core
        summed = jnp.dot(
            weights[i, :, LANES : LANES + keys], tiles[0:keys, :], preferred_element_type=F32
        )
        summed += jnp.dot(
            weights[i, :, 0:LANES],
            v_all[shard].reshape(rows, LANES),
            preferred_element_type=F32,
        )
        o_stage[i] = (summed * totals[i]).astype(BF16)

    @pl.loop(0, heads)
    def _(n):
        i = (mine + 5 * n) % heads
        shard = my_half * middle + 2 * i + core

        @pl.when(my_half == 0)
        def _():
            attend(i, middle)

        @pl.when(my_half == 1)
        def _():
            attend(i, shards)

        @pl.when(shard != me)
        def _():
            remote(
                o_stage.at[i], o_recv.at[mine], o_send.at[i], o_recv_sem.at[mine], seq=shard
            ).start()

        @pl.when(shard == me)
        def _():
            pltpu.make_async_copy(o_stage.at[i], o_recv.at[mine], o_recv_sem.at[mine]).start()

    @pl.loop(0, heads)
    def _(n):
        h = (my_row + heads - n) % heads
        drain(o_recv.at[h], o_recv_sem.at[h])
        cols = columns(h)
        out_v[:, cols] = (stream[h] + o_recv[h].astype(F32)).astype(BF16)

    written = pltpu.make_async_copy(out_v, out, out_sem)
    written.start()

    drain(ends.at[pl.ds(0, LEVEL - 1)], st_send)
    drain(st_out.at[pl.ds(0, LEVEL - 1)], back_send)
    drain(sq.at[pl.ds(0, planes - 1)], sq_send)
    drain(rd_all.at[pl.ds(0, heads - 1)], rd_send)
    drain(q_all.at[pl.ds(0, heads - 1)], q_send)
    drain(q_all.at[pl.ds(0, heads - 1)], k_send)
    drain(q_all.at[pl.ds(0, heads - 1)], v_send)

    @pl.loop(level_at + 1, levels)
    def _(to):
        drain(level, level_send.at[to])

    @pl.when(jnp.logical_not(held_here))
    def _():
        drain(q_all.at[0], own_sem.at[0])
        drain(q_all.at[0], own_sem.at[3])

    @pl.when(jnp.logical_not(at_home))
    def _():
        drain(q_all.at[0], own_sem.at[1])
        drain(rd_all.at[0], own_sem.at[2])

    for fwd in (kf_send, vf_send):

        @pl.when(my_half == 0)
        def _():
            drain(k_all.at[pl.ds(0, 3 * early)], fwd)

        @pl.when(my_half == 1)
        def _():
            drain(k_all.at[pl.ds(0, 5 * early)], fwd)

    @pl.loop(0, heads)
    def _(i):
        @pl.when(my_half * middle + 2 * i + core != me)
        def _():
            drain(o_stage.at[i], o_send.at[i])

    written.wait()


def local(
    shards,
    planes,
    residual,
    hyena_q,
    hyena_k,
    hyena_v,
    modal_residue,
    decay_rate,
    skip_gain,
    attn_q,
    attn_k,
    norm_gain,
    readers,
):
    rows, features = residual.shape
    modes = modal_residue.shape[1]
    ltiles = features // LANES
    heads = shards // GROUP

    hbm = pl.BlockSpec(memory_space=pl.ANY)
    dma = pltpu.SemaphoreType.DMA
    tiled = (rows // TILE, TILE, features)
    block = (rows // TILE, TILE, LANES)
    share = (modes * ltiles // LEVEL, LANES)
    return pl.pallas_call(
        functools.partial(kernel, shards, planes, modes),
        out_shape=jax.ShapeDtypeStruct((rows, features), BF16),
        in_specs=[hbm] * 11,
        out_specs=hbm,
        scratch_shapes=[
            pltpu.VMEM((modes, features), F32),
            pltpu.VMEM((modes, features), F32),
            pltpu.VMEM((ltiles, LANES), F32),
            pltpu.VMEM((ltiles, LANES), F32),
            pltpu.VMEM((1, shards), jnp.int32),
            pltpu.VMEM((rows, features), BF16),
            pltpu.VMEM((rows, features), BF16),
            pltpu.VMEM((rows, features), BF16),
            pltpu.VMEM((rows, features), BF16),
            pltpu.VMEM((2, ltiles * modes, LANES), F32),
            pltpu.VMEM((modes * ltiles, LANES), F32),
            pltpu.VMEM((modes * ltiles, LANES), F32),
            pltpu.VMEM((modes * ltiles, LANES), F32),
            pltpu.VMEM((ltiles * rows, LANES), F32),
            pltpu.VMEM((ltiles * rows, LANES), F32),
            pltpu.VMEM((LEVEL,) + share, F32),
            pltpu.VMEM((LEVEL,) + share, F32),
            pltpu.VMEM(share, F32),
            pltpu.VMEM((shards // LEVEL,) + share, F32),
            pltpu.VMEM((LEVEL,) + share, F32),
            pltpu.VMEM((LEVEL,) + share, F32),
            pltpu.VMEM((ltiles, rows, LANES), F32),
            pltpu.VMEM((planes, 8, LANES), F32),
            pltpu.VMEM((heads,) + block, BF16),
            pltpu.VMEM((heads,) + block, BF16),
            pltpu.VMEM((shards,) + block, BF16),
            pltpu.VMEM((shards,) + block, BF16),
            pltpu.VMEM((2, LANES), jnp.int32),
            pltpu.VMEM((heads, 2, LANES), jnp.int32),
            pltpu.SMEM((heads, 2, LANES), jnp.int32),
            pltpu.VMEM((shards * TILE, LANES), BF16),
            pltpu.VMEM((heads, rows, shards * TILE + rows), BF16),
            pltpu.VMEM((heads, rows, LANES), F32),
            pltpu.VMEM((heads, rows, LANES), BF16),
            pltpu.VMEM((heads, rows, LANES), BF16),
            pltpu.VMEM((rows, features), BF16),
            dma((10,)),
            dma((4,)),
            dma,
            dma,
            dma((shards // LEVEL,)),
            dma((shards // LEVEL,)),
            dma,
            dma,
            dma,
            dma,
            dma,
            dma((heads,)),
            dma,
            dma((heads,)),
            dma,
            dma((shards,)),
            dma,
            dma((shards,)),
            dma,
            dma,
            dma((heads,)),
            dma((heads,)),
            dma,
        ],
        compiler_params=pltpu.CompilerParams(
            collective_id=0, has_side_effects=True, vmem_limit_bytes=60 * 1024 * 1024
        ),
    )(
        residual,
        hyena_q,
        hyena_k,
        hyena_v,
        modal_residue.T,
        decay_rate.T,
        skip_gain.reshape(ltiles, LANES),
        attn_q.reshape(tiled),
        attn_k.reshape(tiled),
        norm_gain.reshape(ltiles, LANES),
        readers,
    )


def solution(mesh):
    spread = P("seq", "chan")
    placed = (
        spread,
        spread,
        spread,
        spread,
        P("chan", None),
        P("chan", None),
        P("chan"),
        spread,
        spread,
        P("chan"),
        P("seq", None),
    )
    return jax.shard_map(
        functools.partial(local, mesh.shape["seq"], mesh.shape["chan"]),
        mesh=mesh,
        in_specs=placed,
        out_specs=spread,
        check_vma=False,
    )
```

time: 109 us -> 91 us (0.83)
  the two profiles are of different devices: /device:TPU:1 before, /device:TPU:65 now
where the time goes in v2:
time: 91 us; the launch traced here: 90.9 us
  Pallas kernels  89 us (98%)
  local copies, waits for them, and re-layouts  1.88 us (2%)
    pallas_call x1, Pallas kernels, local(): pl.pallas_call(functools.partial(kernel, shards, planes, modes), out_shap...  89 us
    unnamed x1, local copies, waits for them, and re-layouts  1.88 us

profile of v2, /device:TPU:65, one launch (start us, length us, event | category | flops | bytes accessed | tf_op | source)
XLA Modules:
  0.0 90.9 jit_solution(3398556926544584466)
XLA Ops:
  0.0 89.0 %shard_map.109 = bf16[128,2048]{1,0:T(8,128)(2,1)} custom-call(bf16[128,2048]{1,0:T(8,128)(2,1)} %residual.1, bf16[128,2048]{1,0:T(8,128)(2,1)} %hyena_q.1, bf16[128,2048]{1,0:T(8,128)(2,1)} %hyena_k.1, bf16[128,2048]{1,0:T(8,128)(2,1)} %hyena_v.1, f32[16,2048]{1,0:T(8,128)} %bitcast.8, f32[16,2048]{1,0:T(8,128)} %bitcast.9, f32[16,128]{1,0:T(8,128)} %bitcast.10, ...), custom_call_target="tpu_custom_call" | custom-call | tf_op jit(solution)/shard_map/pallas_call | solution.py:687
  89.0 1.9 %copy.13 = bf16[128,2048]{1,0:T(8,128)(2,1)} copy(bf16[128,2048]{1,0:T(8,128)(2,1)} %shard_map.109) | data formatting | bytes 1048576

commit v3 on v2

--- a/solution.py
+++ b/solution.py
@@ -12,8 +12,9 @@
 TILE = 16
 GROUP = 4
 LEVEL = 8
-SHARE_LAG = 5
-BLOCKS_AT = (3, 1, 3, 3, 6)
+SHARE_LAG = 4
+VALUES_AHEAD = 15
+BLOCKS_AT = (4, 1, 4, 6, 6)
 F32 = jnp.float32
 BF16 = jnp.bfloat16
 
@@ -249,6 +250,7 @@
 
     pl.semaphore_wait(barrier, LEVEL // 2 + planes - 1 + middle - 1)
     at_entry, at_stretch, at_share, at_level, at_back = BLOCKS_AT
+    keep_key()
     send_blocks(0, at_entry)
     issued = at_entry
 
@@ -370,13 +372,72 @@
     start[place] = st_out[place]
     send_blocks(issued, issued + at_back)
     issued += at_back
-    keep_key()
     loads[5].wait()
     loads[6].wait()
     loads[7].wait()
     loads[8].wait()
     drain(start.at[pl.ds(0, LEVEL - 1)], back_recv)
 
+    early = heads // 2
+
+    def sharing(everything, recv, fwd):
+        def pass_on(slot, to):
+            remote(everything.at[slot], everything.at[slot], fwd, recv.at[slot], seq=to).start()
+
+        def share_slot(slot, to_chip):
+            drain(everything.at[slot], recv.at[slot])
+            if to_chip:
+                pass_on(slot, chip_peer)
+            pass_on(slot, core_peer)
+
+        def share_far(n):
+            slot = n * GROUP + 2 * (1 - side) + core
+            share_slot(slot, False)
+
+        def share_from(n):
+            group = (mine + heads - order(n)) % heads
+
+            @pl.when(group < early)
+            def _():
+                share_slot(group * GROUP + 2 * side + core, True)
+
+            @pl.when(jnp.logical_and(group >= early, my_half == 1))
+            def _():
+                share_slot(group * GROUP + core, False)
+                share_slot(group * GROUP + 2 + core, False)
+
+        def share_step(k):
+            near = (k + mine) % early
+
+            @pl.when(k < early)
+            def _():
+                share_slot(near * GROUP + 2 * side + core, True)
+
+            @pl.when(jnp.logical_and(k >= early, k < 2 * early))
+            def _():
+                share_far(near)
+
+            @pl.when(jnp.logical_and(k >= 2 * early, my_half == 1))
+            def _():
+                share_slot((early + near) * GROUP + core, False)
+                share_slot((early + near) * GROUP + 2 + core, False)
+
+        def arrive():
+            @pl.loop(0, middle // 2)
+            def _(n):
+                slot = 2 * n + 1 - core
+                drain(everything.at[slot], recv.at[slot])
+
+            @pl.when(my_half == 1)
+            def _():
+                @pl.loop(middle // 2, middle)
+                def _(n):
+                    slot = 2 * n + 1 - core
+                    drain(everything.at[slot], recv.at[slot])
+
+        return share_from, share_step, share_far, arrive
+
+    key_from, _, far_key, keys_arrive = sharing(k_all, k_recv, kf_send)
     for part in range(parts):
         base = part * 8 * rows
         skip = skip_ref[part * 8 : part * 8 + 8, :]
@@ -395,6 +456,10 @@
         first = tuple(start[m // per_place, share_rows(m, part), :] for m in range(modes))
 
         lax.fori_loop(0, rows, filtered, first, unroll=4)
+        steps = heads // parts
+        pl.loop(part * steps, (part + 1) * steps)(key_from)
+        left = 2 * (heads - 1) - issued
+        send_blocks(issued + left * part // parts, issued + left * (part + 1) // parts)
 
     def streamed(lt, acc):
         cols = columns(lt)
@@ -414,54 +479,7 @@
     for d in range(1, planes):
         to = (plane + d) % planes
         remote(sq.at[plane], sq.at[plane], sq_send, sq_recv, chan=to).start()
-    send_blocks(issued, 2 * (heads - 1))
     keep_query()
-
-    early = heads // 2
-
-    def sharing(everything, recv, fwd):
-        def pass_on(slot, to):
-            remote(everything.at[slot], everything.at[slot], fwd, recv.at[slot], seq=to).start()
-
-        def share_slot(slot, to_chip):
-            drain(everything.at[slot], recv.at[slot])
-            if to_chip:
-                pass_on(slot, chip_peer)
-            pass_on(slot, core_peer)
-
-        def share_far(n):
-            slot = n * GROUP + 2 * (1 - side) + core
-            share_slot(slot, False)
-
-        def share_from(n):
-            group = (mine + heads - order(n)) % heads
-
-            @pl.when(group < early)
-            def _():
-                share_slot(group * GROUP + 2 * side + core, True)
-
-            @pl.when(jnp.logical_and(group >= early, my_half == 1))
-            def _():
-                share_slot(group * GROUP + core, False)
-                share_slot(group * GROUP + 2 + core, False)
-
-        def arrive():
-            @pl.loop(0, middle // 2)
-            def _(n):
-                slot = 2 * n + 1 - core
-                drain(everything.at[slot], recv.at[slot])
-
-            @pl.when(my_half == 1)
-            def _():
-                @pl.loop(middle // 2, middle)
-                def _(n):
-                    slot = 2 * n + 1 - core
-                    drain(everything.at[slot], recv.at[slot])
-
-        return share_from, share_far, arrive
-
-    key_from, far_key, keys_arrive = sharing(k_all, k_recv, kf_send)
-    pl.loop(0, heads)(key_from)
 
     def far_keys():
         pl.loop(0, early)(far_key)
@@ -477,12 +495,12 @@
         value = stream[h] * scale * gain_ref[pl.ds(h, 1), :]
         return value.astype(BF16).reshape(rows // TILE, TILE, LANES)
 
-    @pl.loop(0, heads - 1)
-    def _(n):
+    def send_value(n):
         h = (mine + order(n)) % heads
         vloc[h] = normed(h)
         remote(vloc.at[h], v_all.at[me], v_send, v_recv.at[me], seq=holder_of(h)).start()
 
+    pl.loop(0, VALUES_AHEAD)(send_value)
     vloc[mine] = normed(mine)
 
     @pl.when(held_here)
@@ -546,15 +564,20 @@
         total = jnp.sum(total, axis=1, keepdims=True)
         totals[i] = jnp.broadcast_to(1.0 / total, (rows, LANES))
 
-    share_from, share_far, arrive = sharing(v_all, v_recv, vf_send)
+    _, share_step, _, arrive = sharing(v_all, v_recv, vf_send)
 
     @pl.loop(0, heads)
     def _(n):
         drain(q_all.at[n], q_recv.at[n])
 
+        @pl.when(n < heads - 1 - VALUES_AHEAD)
+        def _():
+            send_value(n + VALUES_AHEAD)
+
         @pl.when(n >= SHARE_LAG)
         def _():
-            share_from(n - SHARE_LAG)
+            share_step(2 * (n - SHARE_LAG))
+            share_step(2 * (n - SHARE_LAG) + 1)
 
         @pl.when(my_half == 0)
         def _():
@@ -564,11 +587,7 @@
         def _():
             weigh(n, shards)
 
-    @pl.loop(heads - SHARE_LAG, heads)
-    def _(n):
-        share_from(n)
-
-    pl.loop(0, early)(share_far)
+    pl.loop(2 * (heads - SHARE_LAG), 3 * early)(share_step)
     arrive()
 
     def attend(i, count):

time: 91 us -> 85.2 us (0.936)
  the two profiles are of different devices: /device:TPU:65 before, /device:TPU:1 now
where the time goes in v3:
time: 85.2 us; the launch traced here: 84.3 us
  Pallas kernels  82.4 us (97%)
  local copies, waits for them, and re-layouts  1.88 us (2%)
    pallas_call x1, Pallas kernels, local(): pl.pallas_call(functools.partial(kernel, shards, planes, modes), out_shap...  82.4 us
    unnamed x1, local copies, waits for them, and re-layouts  1.88 us

profile of v3, /device:TPU:1, one launch (start us, length us, event | category | flops | bytes accessed | tf_op | source)
XLA Modules:
  0.0 84.3 jit_solution(15354553791941185317)
XLA Ops:
  0.0 82.4 %shard_map.109 = bf16[128,2048]{1,0:T(8,128)(2,1)} custom-call(bf16[128,2048]{1,0:T(8,128)(2,1)} %residual.1, bf16[128,2048]{1,0:T(8,128)(2,1)} %hyena_q.1, bf16[128,2048]{1,0:T(8,128)(2,1)} %hyena_k.1, bf16[128,2048]{1,0:T(8,128)(2,1)} %hyena_v.1, f32[16,2048]{1,0:T(8,128)} %bitcast.8, f32[16,2048]{1,0:T(8,128)} %bitcast.9, f32[16,128]{1,0:T(8,128)} %bitcast.10, ...), custom_call_target="tpu_custom_call" | custom-call | tf_op jit(solution)/shard_map/pallas_call | solution.py:706
  82.4 1.9 %copy.13 = bf16[128,2048]{1,0:T(8,128)(2,1)} copy(bf16[128,2048]{1,0:T(8,128)(2,1)} %shard_map.109) | data formatting | bytes 1048576

commit v4 on v3

--- a/solution.py
+++ b/solution.py
@@ -633,9 +633,8 @@
         drain(o_recv.at[h], o_recv_sem.at[h])
         cols = columns(h)
         out_v[:, cols] = (stream[h] + o_recv[h].astype(F32)).astype(BF16)
-
-    written = pltpu.make_async_copy(out_v, out, out_sem)
-    written.start()
+        pltpu.make_async_copy(out_v.at[:, cols], out.at[:, cols], out_sem).start()
+
 
     drain(ends.at[pl.ds(0, LEVEL - 1)], st_send)
     drain(st_out.at[pl.ds(0, LEVEL - 1)], back_send)
@@ -675,7 +674,7 @@
         def _():
             drain(o_stage.at[i], o_send.at[i])
 
-    written.wait()
+    drain(out_v, out_sem)
 
 
 def local(

time: 85.2 us -> 85.1 us (level)
  no operation moved by 1% of the time
where the time goes in v4:
time: 85.1 us; the launch traced here: 84.1 us
  Pallas kernels  82.2 us (97%)
  local copies, waits for them, and re-layouts  1.88 us (2%)
    pallas_call x1, Pallas kernels, local(): pl.pallas_call(functools.partial(kernel, shards, planes, modes), out_shap...  82.2 us
    unnamed x1, local copies, waits for them, and re-layouts  1.88 us

profile of v4, /device:TPU:1, one launch (start us, length us, event | category | flops | bytes accessed | tf_op | source)
XLA Modules:
  0.0 84.1 jit_solution(5941305177096345970)
XLA Ops:
  0.0 82.2 %shard_map.109 = bf16[128,2048]{1,0:T(8,128)(2,1)} custom-call(bf16[128,2048]{1,0:T(8,128)(2,1)} %residual.1, bf16[128,2048]{1,0:T(8,128)(2,1)} %hyena_q.1, bf16[128,2048]{1,0:T(8,128)(2,1)} %hyena_k.1, bf16[128,2048]{1,0:T(8,128)(2,1)} %hyena_v.1, f32[16,2048]{1,0:T(8,128)} %bitcast.8, f32[16,2048]{1,0:T(8,128)} %bitcast.9, f32[16,128]{1,0:T(8,128)} %bitcast.10, ...), custom_call_target="tpu_custom_call" | custom-call | tf_op jit(solution)/shard_map/pallas_call | solution.py:705
  82.3 1.9 %copy.13 = bf16[128,2048]{1,0:T(8,128)(2,1)} copy(bf16[128,2048]{1,0:T(8,128)(2,1)} %shard_map.109) | data formatting | bytes 1048576
